TPU v7x, 256 devices: a whole 4x4x8 slice. The times are simulated.
256 devices in a mesh: blk: 16 (over x_hi, y, core), tm: 16 (over z, x_lo).
Axes of the slice: x: 4 (x_hi: 2, x_lo: 2; x = x_hi * 2 + x_lo), y: 4, z: 8, core: 2. Of those that a mesh axis runs over, the one named last changes fastest.
Arguments:
- occupied_orbitals: float32 [2048, 2048], P(None, 'blk'), may hold values from -0.6 to 0.6
- empty_orbitals: float32 [2048, 2048], P(None, 'blk'), may hold values from -0.6 to 0.6
- occupied_energy: float32 [2048], replicated, may hold values from -1.5 to -0.05
- empty_energy: float32 [2048], replicated, may hold values from 0.05 to 1.5
- time_points: float32 [16], replicated, may hold values from 0.25 to 4
- pair_table: int32 [16], replicated, may hold values from 0 to 15, each once
Outputs:
- polarizability: float32 [16, 2, 2048, 1024], P('tm', None, 'blk')
Inputs may be any that keep to these rules, and one draw needn't show every extreme that they name: `pair_table`: each of 0 to 15 appears exactly once.
All inputs are finite; a program needn't handle non-finite values.
Results may differ from a plain program's by a relative error of at most 0.000088.
Values sent between devices are 32-bit elements; how exact they have to be, the bound alone decides.
A program may use at most 64 MiB of HBM per device.

v0:
```python
import jax
import jax.numpy as jnp
from jax import lax
from jax.sharding import PartitionSpec as P

TAU_DEV = 2


def swapped(value, axis, apart):
    mask = 2**apart
    pairs = [(source, source ^ mask) for source in range(lax.axis_size(axis))]
    return lax.ppermute(value, axis, pairs)


def body(occupied_orbitals, empty_orbitals, occupied_energy, empty_energy, time_points, pair_table):
    slot_count = TAU_DEV
    points_own = occupied_orbitals.shape[1]
    cycle_size = lax.axis_size("blk")
    total_points = points_own * cycle_size
    time_index = lax.axis_index("tm")
    pair_index = time_index // 2
    half_index = time_index % 2
    is_empty = half_index == 0
    orbitals = jnp.where(is_empty, empty_orbitals, occupied_orbitals)
    energy = jnp.where(is_empty, -empty_energy, occupied_energy)
    slots = pair_index * slot_count + jnp.arange(slot_count, dtype=jnp.int32)
    moments = time_points[pair_table[slots]]
    weights = jnp.exp(energy[None, :] * moments[:, None])
    weighted = orbitals[None, :, :] * weights[:, :, None]
    green_tile = jnp.einsum(
        "tsp,sq->tpq",
        weighted,
        lax.all_gather(orbitals, "blk", axis=1, tiled=True),
        precision=lax.Precision.HIGHEST,
        preferred_element_type=jnp.float32,
    )
    half_width = total_points // 2
    left_half = green_tile[:, :, :half_width]
    right_half = green_tile[:, :, half_width:]
    outgoing = jnp.where(is_empty, right_half, left_half)
    kept_half = jnp.where(is_empty, left_half, right_half)
    incoming = swapped(outgoing, "tm", 0)
    product = -(kept_half * incoming)
    return product[None]


def solution(mesh):
    return jax.shard_map(
        body,
        mesh=mesh,
        in_specs=(P(None, "blk"), P(None, "blk"), P(), P(), P(), P()),
        out_specs=P("tm", None, "blk", None),
        check_vma=False,
    )
```

profile of v0, /device:TPU:3, one launch (start us, length us, event | category | flops | bytes accessed | tf_op | source)
XLA Modules:
  0.0 186.6 jit_solution(11896620606444321976)
XLA Ops:
  6.5 0.0 copy-start
  6.5 0.0 all-gather.2.cloned.1.call-start
  6.5 2.3 %broadcast_select_fusion = f32[2048,128]{1,0:T(8,128)} fusion(f32[2048,128]{1,0:T(8,128)} %param.7, f32[2048,128]{1,0:T(8,128)} %param.6, pred[]{:T(512)S(6)} %eq.5), kind=kLoop, calls=%fused_computation.9 | loop fusion | flops 262144 | bytes 3145729 | tf_op jit(solution)/shard_map/jit(_where)/select_n | solution.py:24
  8.9 0.0 copy-start.1
  8.9 0.0 copy-start.2
  8.9 0.0 copy-start.3
  8.9 0.0 all-gather.2.cloned.1.call-update
  8.9 1.6 copy.8
  10.5 0.0 copy-done
  10.5 0.6 gather_fusion
  11.2 0.0 copy-done.1
  11.2 0.6 gather_fusion.1
  11.8 0.0 copy-done.2
  11.8 0.0 copy-done.3
  11.8 0.1 multiply_exponential_fusion
  11.9 124.5 %all-gather.2.cloned.1.call-done = f32[2048,2048]{1,0:T(8,128)} async-done(((f32[2048,128]{1,0:T(8,128)}), f32[2048,2048]{1,0:T(8,128)}) %all-gather.2.cloned.1.call-update) | async-done | bytes 16777232 | tf_op jit(solution)/shard_map/all_gather | solution.py:33
  136.4 17.3 %fusion = f32[2,128,2048]{2,1,0:T(8,128)S(1)} fusion(f32[2048,2048]{1,0:T(8,128)} %all-gather.2.cloned.1.call-done, f32[2,2048]{1,0:T(2,128)S(1)} %multiply_exponential_fusion, f32[2048,128]{0,1:T(8,128)S(1)} %copy.8), kind=kOutput, calls=%fused_computation.2 | convolution fusion | flops 12885426176 | bytes 19939328 | tf_op jit(solution)/shard_map/tsp,sq->tpq/dot_general | solution.py:30
  153.7 0.1 slice_select_fusion
  153.8 1.3 collective-permute-start
  155.1 23.3 %collective-permute-done = f32[2,128,1024]{2,1,0:T(8,128)S(1)} collective-permute-done((f32[2,128,1024]{2,1,0:T(8,128)S(1)}, f32[2,128,1024]{2,1,0:T(8,128)S(1)}, u32[]{:S(2)}, u32[]{:S(2)}) %collective-permute-start) | collective-permute-done | bytes 1048608 | tf_op jit(solution)/shard_map/ppermute | solution.py:12
  178.4 1.3 negate_bitcast_fusion
  (5 shorter events, 0.0 us)
Async XLA Ops:
  6.5 4.0 %copy-start = (s32[16]{0:T(128)S(1)}, s32[16]{0:T(128)}, u32[]{:S(2)}) copy-start(s32[16]{0:T(128)} %param.11) | copy-start | bytes 196
  6.5 129.9 %all-gather.2.cloned.1.call-start = ((), (), s32[]{:S(2)}) async-start(), calls=%async_computation | async-start | bytes 17825792 | tf_op jit(solution)/shard_map/all_gather | solution.py:33
  8.9 2.3 %copy-start.1 = (f32[16]{0:T(128)S(1)}, f32[16]{0:T(128)}, u32[]{:S(2)}) copy-start(f32[16]{0:T(128)} %param.10) | copy-start | bytes 196
  8.9 3.0 %copy-start.2 = (f32[2048]{0:T(1024)S(1)}, f32[2048]{0:T(1024)}, u32[]{:S(2)}) copy-start(f32[2048]{0:T(1024)} %param.8) | copy-start | bytes 24580
  8.9 3.0 %copy-start.3 = (f32[2048]{0:T(1024)S(1)}, f32[2048]{0:T(1024)}, u32[]{:S(2)}) copy-start(f32[2048]{0:T(1024)} %param.9) | copy-start | bytes 24580
  153.8 24.6 %collective-permute-start = (f32[2,128,1024]{2,1,0:T(8,128)S(1)}, f32[2,128,1024]{2,1,0:T(8,128)S(1)}, u32[]{:S(2)}, u32[]{:S(2)}) collective-permute-start(f32[2,128,1024]{2,1,0:T(8,128)S(1)} %slice_select_fusion), channel_id=1, source_target_pairs={{0,1},{1,0},{2,3},{3,2},{4,5},{5,4},{6,7},{7,6},{8,9},{9,8},{10,11... | collective-permute-start | bytes 3145736 | tf_op jit(solution)/shard_map/ppermute | solution.py:12
Sparse Core Ops, SparseCore 0:
  9.9 126.4 all-gather.1
where the time goes:
time: 188 us; the launch traced here: 187 us
  waiting for transfers between devices  148 us (79%)
  matrix products  17.3 us (9%)
  between operations  13.5 us (7%)
  other arithmetic  3.84 us (2%)
  local copies, waits for them, and re-layouts  2.86 us (2%)
    all_gather x1, waiting for transfers between devices, body(): lax.all_gather(orbitals, 'blk', axis=1, tiled=True)  124 us
    ppermute x1, waiting for transfers between devices, swapped(): return lax.ppermute(value, axis, pairs)  23.3 us
    dot_general x1, matrix products, body(): jnp.einsum('tsp,sq->tpq', weighted, lax.all_gather(orbitals, 'blk', axis=...  17.3 us
  transfers between devices with their start and end apart: 2, of which 2 were waited for; matrix products, arithmetic and copies ran while one was open for 2% of the time, Pallas kernels for 0%

commit v1 on v0

v1 whole, which is shorter than its diff:
```python
import jax
import jax.numpy as jnp
from jax import lax
from jax.experimental import pallas as pl
from jax.experimental.pallas import tpu as pltpu
from jax.sharding import PartitionSpec as P

MESH = pl.DeviceIdType.MESH
NZ = 8
NY = 4
F32 = jnp.float32
BF16 = jnp.bfloat16


def split(value):
    hi = value.astype(BF16)
    lo = (value - hi.astype(F32)).astype(BF16)
    return hi, lo


def kernel(occ_ref, emp_ref, occ_e_ref, emp_e_ref, time_ref, pair_ref, out_ref,
           turned, own, slices, rhs, lhs, weights, outgoing, arrived, result,
           ag_send, ag_recv, z_send, z_recv, mirror_send, mirror_recv, out_sem):
    states, width = occ_ref.shape
    piece = width // NZ
    blk, tm = lax.axis_index("blk"), lax.axis_index("tm")
    x_hi, y, c = lax.div(blk, 8), lax.rem(lax.div(blk, 2), NY), lax.rem(blk, 2)
    z, half = lax.div(tm, 2), lax.rem(tm, 2)
    home = x_hi == half
    column = lax.rem(blk, 8)

    def in_column(y_to, c_to):
        return (x_hi * 8 + lax.rem(y_to, NY) * 2 + c_to, tm)

    sibling = in_column(y, 1 - c)
    up, down = in_column(y + 1, c), in_column(y + 3, c)
    across = (half * 8 + y * 2 + c, z * 2 + x_hi)

    def z_peer(step):
        return (blk, lax.rem(z + step, NZ) * 2 + half)

    def block_of(q):
        group, flip = lax.div(q, 2), lax.rem(q, 2)
        dy = group ^ lax.div(group, 2)
        return half * 8 + lax.rem(y + dy, NY) * 2 + lax.rem(c + flip, 2)

    def mirror_of(q):
        return (block_of(q), z * 2 + x_hi)

    barrier = pltpu.get_barrier_semaphore()

    def greet(device):
        pl.semaphore_signal(barrier, inc=1, device_id=device, device_id_type=MESH)

    @pl.loop(1, NZ)
    def _(step):
        greet(z_peer(step))

    @pl.loop(1, 8)
    def _(q):
        greet(mirror_of(q))

    @pl.when(jnp.logical_not(home))
    def _():
        greet(across)
        greet(sibling)
        greet(up)
        greet(down)

    rows = lax.broadcasted_iota(jnp.int32, (16, 1), 0)
    moments = jnp.zeros((16, 1), F32)
    for row in range(16):
        moment = time_ref[pair_ref[2 * (row % 8) + row // 8]]
        moments = jnp.where(rows == row, moment, moments)
    weights[0] = jnp.exp(-emp_e_ref[...] * moments)
    weights[1] = jnp.exp(occ_e_ref[...] * moments)

    for kind, ref in enumerate((emp_ref, occ_ref)):
        @pl.loop(0, states // 256)
        def _(chunk):
            at = pl.ds(pl.multiple_of(chunk * 256, 256), 256)
            turned[kind, :, at] = ref[at, :].T
    own[...] = turned[:, pl.ds(pl.multiple_of(z * piece, piece), piece), :]

    @pl.when(home)
    def _():
        slices[0] = own[...]
        pl.semaphore_wait(barrier, 14)

    def gather_copy(source, at, device, n):
        return pltpu.make_async_remote_copy(
            src_ref=source, dst_ref=slices.at[at], send_sem=ag_send.at[n], recv_sem=ag_recv.at[at],
            device_id=device, device_id_type=MESH)

    cross = gather_copy(own, 0, across, 0)
    to_sibling = gather_copy(slices.at[0], 1, sibling, 1)
    to_up = gather_copy(slices.at[0], 4, up, 2)
    to_down = gather_copy(slices.at[0], 2, down, 3)

    @pl.when(jnp.logical_not(home))
    def _():
        pl.semaphore_wait(barrier, 18)
        cross.start()

    for kind, ref in enumerate((emp_ref, occ_ref)):
        @pl.loop(0, states // 256)
        def _(chunk):
            at = pl.ds(pl.multiple_of(chunk * 256, 256), 256)
            hi, lo = split(ref[at, :])
            rhs[kind, at, 0:width] = hi
            rhs[kind, at, width:] = lo

    @pl.when(jnp.logical_not(home))
    def _():
        cross.wait_recv()

    to_up.start()
    to_down.start()
    to_sibling.start()

    def z_copy(q, step):
        to = lax.rem(z + step, NZ)
        return pltpu.make_async_remote_copy(
            src_ref=outgoing.at[q, to], dst_ref=arrived.at[q, pl.ds(pl.multiple_of(z * piece, piece), piece)],
            send_sem=z_send.at[q], recv_sem=z_recv.at[q], device_id=z_peer(step), device_id_type=MESH)

    def compute(q, at, u):
        tiles = []
        for kind in range(2):
            values = slices[q, kind]
            for p in range(8):
                factor = weights[kind, pl.ds(pl.multiple_of(u * 8, 8), 8), :][p:p + 1, :]
                hi, lo = split(values * factor)
                lhs[kind, p * piece:(p + 1) * piece, :] = hi
                lhs[kind, 128 + p * piece:128 + (p + 1) * piece, :] = lo
            total = jnp.dot(lhs[kind], rhs[kind], preferred_element_type=F32)
            tiles.append((total[0:128, 0:width]
                          + (total[0:128, width:] + (total[128:, 0:width] + total[128:, width:]))))
        outgoing[at] = (-(tiles[0] * tiles[1])).reshape(8, piece, width)
        arrived[at, pl.ds(pl.multiple_of(z * piece, piece), piece), :] = outgoing[at, z]

        @pl.loop(1, NZ)
        def _(step):
            z_copy(at, step).start()

    def slot_of(q):
        return (block_of(q) < blk).astype(jnp.int32)

    def gathered(q):
        gather_copy(slices.at[q], q, sibling, 0).wait_recv()

    def receive(q):
        rest = arrived.at[q, pl.ds(0, (NZ - 1) * piece)]
        pltpu.make_async_copy(rest, rest, z_recv.at[q]).wait()

    def mirror_copy(q):
        return pltpu.make_async_remote_copy(
            src_ref=arrived.at[q], dst_ref=result.at[slot_of(q), :, pl.ds(pl.multiple_of(column * width, width), width)],
            send_sem=mirror_send.at[q], recv_sem=mirror_recv.at[column], device_id=mirror_of(q), device_id_type=MESH)

    def place(q, at, u):
        columns = pl.ds(pl.multiple_of(lax.rem(block_of(q), 8) * width, width), width)
        result[u, :, columns] = arrived[at].T

    def finish(q):
        receive(q)
        mirror_copy(q).start()
        place(q, q, slot_of(q))

    compute(0, 0, slot_of(0))

    @pl.when(home)
    def _():
        compute(0, 8, 1)

    gathered(1)
    compute(1, 1, slot_of(1))

    gathered(2)
    past_up = gather_copy(slices.at[2], 3, sibling, 4)
    past_up.start()
    gathered(4)
    past_down = gather_copy(slices.at[4], 5, sibling, 5)
    past_down.start()
    on_down = gather_copy(slices.at[2], 6, down, 6)
    on_up = gather_copy(slices.at[4], 6, up, 6)
    pl.when(c == 1)(on_down.start)
    pl.when(c == 0)(on_up.start)
    gathered(3)
    gathered(5)

    @pl.loop(2, 6)
    def _(q):
        compute(q, q, slot_of(q))

    gathered(6)
    far = gather_copy(slices.at[6], 7, sibling, 7)
    far.start()

    @pl.when(home)
    def _():
        receive(0)
        receive(8)
        place(0, 0, 0)
        place(0, 8, 1)

    @pl.when(jnp.logical_not(home))
    def _():
        finish(0)

    finish(1)
    compute(6, 6, slot_of(6))
    gathered(7)
    compute(7, 7, slot_of(7))

    @pl.loop(2, 8)
    def _(q):
        finish(q)

    def mirror_arrival(k):
        into = result.at[0, :, pl.ds(0, width)]
        pltpu.make_async_copy(into, into, mirror_recv.at[k]).wait()

    @pl.loop(0, 8)
    def _(k):
        @pl.when(jnp.logical_or(jnp.logical_not(home), k != column))
        def _():
            mirror_arrival(k)

    for u in range(2):
        pltpu.make_async_copy(result.at[u], out_ref.at[0, u], out_sem.at[u]).start()

    to_up.wait_send()
    to_down.wait_send()
    to_sibling.wait_send()
    past_up.wait_send()
    past_down.wait_send()
    on_up.wait_send()
    far.wait_send()

    def sent(q):
        rest = outgoing.at[q, pl.ds(0, NZ - 1)]
        pltpu.make_async_copy(rest, rest, z_send.at[q]).wait()

    @pl.loop(0, 8)
    def _(q):
        sent(q)

    @pl.loop(1, 8)
    def _(q):
        mirror_copy(q).wait_send()

    @pl.when(home)
    def _():
        sent(8)

    @pl.when(jnp.logical_not(home))
    def _():
        cross.wait_send()
        mirror_copy(0).wait_send()

    for u in range(2):
        pltpu.make_async_copy(result.at[u], out_ref.at[0, u], out_sem.at[u]).wait()


def body(occupied_orbitals, empty_orbitals, occupied_energy, empty_energy, time_points, pair_table):
    states, width = occupied_orbitals.shape
    piece = width // NZ
    vmem = pl.BlockSpec(memory_space=pltpu.VMEM)
    smem = pl.BlockSpec(memory_space=pltpu.SMEM)
    return pl.pallas_call(
        kernel,
        out_shape=jax.ShapeDtypeStruct((1, 2, width, 8 * width), F32),
        in_specs=[vmem, vmem, vmem, vmem, smem, smem],
        out_specs=pl.BlockSpec(memory_space=pl.ANY),
        scratch_shapes=[
            pltpu.VMEM((2, width, states), F32),
            pltpu.VMEM((2, piece, states), F32),
            pltpu.VMEM((8, 2, piece, states), F32),
            pltpu.VMEM((2, states, 2 * width), BF16),
            pltpu.VMEM((2, 256, states), BF16),
            pltpu.VMEM((2, 16, states), F32),
            pltpu.VMEM((9, NZ, piece, width), F32),
            pltpu.VMEM((9, width, width), F32),
            pltpu.VMEM((2, width, 8 * width), F32),
            pltpu.SemaphoreType.DMA((8,)),
            pltpu.SemaphoreType.DMA((8,)),
            pltpu.SemaphoreType.DMA((9,)),
            pltpu.SemaphoreType.DMA((9,)),
            pltpu.SemaphoreType.DMA((8,)),
            pltpu.SemaphoreType.DMA((8,)),
            pltpu.SemaphoreType.DMA((2,)),
        ],
        compiler_params=pltpu.CompilerParams(
            collective_id=0, has_side_effects=True, vmem_limit_bytes=40 * 2**20),
        cost_estimate=pl.CostEstimate(flops=2**33, bytes_accessed=2**22, transcendentals=2**16),
        name="polarizability",
    )(occupied_orbitals, empty_orbitals, occupied_energy.reshape(1, states), empty_energy.reshape(1, states),
      time_points, pair_table)


def solution(mesh):
    return jax.shard_map(
        body,
        mesh=mesh,
        in_specs=(P(None, "blk"), P(None, "blk"), P(), P(), P(), P()),
        out_specs=P("tm", None, "blk", None),
        check_vma=False,
    )
```

time: 188 us -> 49.2 us (0.26)
  waiting for transfers between devices: 148 us -> 0 us
  Pallas kernels: 0 us -> 43.3 us
  matrix products: 17.3 us -> 0 us
  between operations: 13.5 us -> 0.02 us
  other arithmetic: 3.84 us -> 0 us
  local copies, waits for them, and re-layouts: 2.86 us -> 5.48 us
    all_gather x1 -> x0, waiting for transfers between devices: 124 us -> none  [body(): lax.all_gather(orbitals, 'blk', axis=1, tiled=True)]
    pallas_call x0 -> x1, Pallas kernels: none -> 43.3 us  [body(): pl.pallas_call(kernel, out_shape=jax.ShapeDtypeStruct((1, 2, width, 8 * w...]
    ppermute x1 -> x0, waiting for transfers between devices: 23.3 us -> none  [swapped(): return lax.ppermute(value, axis, pairs)]
    dot_general x1 -> x0, matrix products: 17.3 us -> none  [body(): jnp.einsum('tsp,sq->tpq', weighted, lax.all_gather(orbitals, 'blk', axis=...]
    unnamed x8 -> x13, local copies, waits for them, and re-layouts: 0.02 us -> 5.48 us
    select_n x5 -> x0, other arithmetic: 2.47 us -> none  [the longest x1 2.31 us: body(): orbitals = jnp.where(is_empty, empty_orbitals, occupied_orbitals)]
  transfers between devices with their start and end apart: 2 -> 0, of which waited for: 2 -> 0; matrix products, arithmetic and copies ran while one was open for 2% -> 0% of each run, Pallas kernels for 0% -> 0%
where the time goes in v1:
time: 49.2 us; the launch traced here: 48.8 us
  Pallas kernels  43.3 us (88%)
  local copies, waits for them, and re-layouts  5.48 us (11%)
    pallas_call x1, Pallas kernels, body(): pl.pallas_call(kernel, out_shape=jax.ShapeDtypeStruct((1, 2, width, 8 * w...  43.3 us
    unnamed x13, local copies, waits for them, and re-layouts  5.48 us

profile of v1, /device:TPU:3, one launch (start us, length us, event | category | flops | bytes accessed | tf_op | source)
XLA Modules:
  0.0 48.8 jit_solution(1976099738491737296)
XLA Ops:
  0.0 0.0 copy-start.4
  0.0 0.0 copy-start.5
  0.0 0.7 %copy-done.4 = f32[16]{0:T(128)S(1)} copy-done((f32[16]{0:T(128)S(1)}, f32[16]{0:T(128)}, u32[]{:S(2)}) %copy-start.4) | copy-done | bytes 88
  0.7 0.0 copy-done.5
  0.7 0.0 copy-start
  0.7 1.2 %copy-done = f32[2048,128]{1,0:T(8,128)S(1)} copy-done((f32[2048,128]{1,0:T(8,128)S(1)}, f32[2048,128]{1,0:T(8,128)}, u32[]{:S(2)}) %copy-start) | copy-done | bytes 1048600
  1.9 0.0 copy-start.1
  1.9 1.2 %copy-done.1 = f32[2048,128]{1,0:T(8,128)S(1)} copy-done((f32[2048,128]{1,0:T(8,128)S(1)}, f32[2048,128]{1,0:T(8,128)}, u32[]{:S(2)}) %copy-start.1) | copy-done | bytes 1048600
  3.1 0.0 copy-start.2
  3.1 0.7 %copy-done.2 = f32[2048]{0:T(1024)S(1)} copy-done((f32[2048]{0:T(1024)S(1)}, f32[2048]{0:T(1024)}, u32[]{:S(2)}) %copy-start.2) | copy-done | bytes 8216
  3.8 0.0 copy-start.3
  3.8 0.7 %copy-done.3 = f32[2048]{0:T(1024)S(1)} copy-done((f32[2048]{0:T(1024)S(1)}, f32[2048]{0:T(1024)}, u32[]{:S(2)}) %copy-start.3) | copy-done | bytes 8216
  4.5 43.3 %polarizability.1 = f32[1,2,128,1024]{3,2,1,0:T(8,128)S(1)} custom-call(f32[2048,128]{1,0:T(8,128)S(1)} %copy-done, f32[2048,128]{1,0:T(8,128)S(1)} %copy-done.1, f32[1,2048]{1,0:T(1,128)S(1)} %bitcast.2, f32[1,2048]{1,0:T(1,128)S(1)} %bitcast.3, f32[16]{0:T(128)S(1)} %copy-done.4, s32[16]{0:T(128)S(1)} %copy-done.5), custom_call_target="tpu_custom_call" | custom-call | flops 8589934592 | bytes 4194304 | tf_op jit(solution)/shard_map/polarizability/pallas_call | solution.py:271
  47.8 1.0 %copy.8 = f32[1,2,128,1024]{3,2,1,0:T(8,128)} copy(f32[1,2,128,1024]{3,2,1,0:T(8,128)S(1)} %polarizability.1) | data formatting | bytes 2097152
Async XLA Ops:
  0.0 0.7 %copy-start.4 = (f32[16]{0:T(128)S(1)}, f32[16]{0:T(128)}, u32[]{:S(2)}) copy-start(f32[16]{0:T(128)} %time_ref.1) | copy-start | bytes 196
  0.0 0.7 %copy-start.5 = (s32[16]{0:T(128)S(1)}, s32[16]{0:T(128)}, u32[]{:S(2)}) copy-start(s32[16]{0:T(128)} %pair_ref.1) | copy-start | bytes 196
  0.7 1.2 %copy-start = (f32[2048,128]{1,0:T(8,128)S(1)}, f32[2048,128]{1,0:T(8,128)}, u32[]{:S(2)}) copy-start(f32[2048,128]{1,0:T(8,128)} %occ_ref.1) | copy-start | bytes 3145732
  1.9 1.2 %copy-start.1 = (f32[2048,128]{1,0:T(8,128)S(1)}, f32[2048,128]{1,0:T(8,128)}, u32[]{:S(2)}) copy-start(f32[2048,128]{1,0:T(8,128)} %emp_ref.1) | copy-start | bytes 3145732
  3.1 0.7 %copy-start.2 = (f32[2048]{0:T(1024)S(1)}, f32[2048]{0:T(1024)}, u32[]{:S(2)}) copy-start(f32[2048]{0:T(1024)} %param.8) | copy-start | bytes 24580
  3.8 0.7 %copy-start.3 = (f32[2048]{0:T(1024)S(1)}, f32[2048]{0:T(1024)}, u32[]{:S(2)}) copy-start(f32[2048]{0:T(1024)} %param.9) | copy-start | bytes 24580

commit v2 on v0

v2 whole, which is shorter than its diff:
```python
import jax
import jax.numpy as jnp
from jax import lax
from jax.experimental import pallas as pl
from jax.experimental.pallas import tpu as pltpu
from jax.sharding import PartitionSpec as P

MESH = pl.DeviceIdType.MESH
NZ = 8
NY = 4
PARTS = 4
F32 = jnp.float32
BF16 = jnp.bfloat16


def split(value):
    hi = value.astype(BF16)
    lo = (value - hi.astype(F32)).astype(BF16)
    return hi, lo


def kernel(occ_hbm, emp_hbm, occ_e_hbm, emp_e_hbm, time_hbm, pair_hbm, out_ref,
           blocks, energies, time_ref, pair_ref, own, slices, rhs, lhs, weights, outgoing, arrived,
           load_sem, small_sem, ag_send, ag_recv, z_send, z_recv, mirror_send, mirror_recv):
    states, width = blocks.shape[1:]
    piece = width // NZ
    depth = states // PARTS
    blk, tm = lax.axis_index("blk"), lax.axis_index("tm")
    x_hi, y, c = lax.div(blk, 8), lax.rem(lax.div(blk, 2), NY), lax.rem(blk, 2)
    z, half = lax.div(tm, 2), lax.rem(tm, 2)
    home = x_hi == half
    away = jnp.logical_not(home)
    column = lax.rem(blk, 8)

    def in_column(y_to, c_to):
        return (x_hi * 8 + lax.rem(y_to, NY) * 2 + c_to, tm)

    sibling = in_column(y, 1 - c)
    up, down = in_column(y + 1, c), in_column(y + 3, c)
    across = (half * 8 + y * 2 + c, z * 2 + x_hi)

    def z_peer(step):
        return (blk, lax.rem(z + step, NZ) * 2 + half)

    def block_of(q):
        group, flip = lax.div(q, 2), lax.rem(q, 2)
        dy = group ^ lax.div(group, 2)
        return half * 8 + lax.rem(y + dy, NY) * 2 + lax.rem(c + flip, 2)

    def mirror_of(q):
        return (block_of(q), z * 2 + x_hi)

    loads = []
    for part in range(PARTS):
        rows = pl.ds(part * depth, depth)
        loads.append([pltpu.make_async_copy(ref.at[rows], blocks.at[kind, rows], load_sem.at[part, kind])
                      for kind, ref in enumerate((emp_hbm, occ_hbm))])
    small = [pltpu.make_async_copy(source, to, small_sem.at[n]) for n, (source, to) in enumerate((
        (emp_e_hbm, energies.at[0]), (occ_e_hbm, energies.at[1]), (time_hbm, time_ref), (pair_hbm, pair_ref)))]
    for pair in loads:
        for copy in pair:
            copy.start()
    for copy in small:
        copy.start()

    barrier = pltpu.get_barrier_semaphore()

    def greet(device):
        pl.semaphore_signal(barrier, inc=1, device_id=device, device_id_type=MESH)

    @pl.loop(1, NZ)
    def _(step):
        greet(z_peer(step))

    @pl.loop(1, 8)
    def _(q):
        greet(mirror_of(q))

    @pl.when(away)
    def _():
        greet(across)
        greet(sibling)
        greet(up)
        greet(down)

    def gather_copy(source, at, part, device, n):
        return pltpu.make_async_remote_copy(
            src_ref=source.at[part], dst_ref=slices.at[at, part], send_sem=ag_send.at[n],
            recv_sem=ag_recv.at[at, part if at % 2 == 0 else 0], device_id=device, device_id_type=MESH)

    def cross(part):
        return gather_copy(own, 0, part, across, 0)

    def spread(part):
        for at, device, n in ((4, up, 1), (2, down, 2), (1, sibling, 3)):
            gather_copy(slices.at[0], at, part, device, n).start()

    for part in range(PARTS):
        for kind in range(2):
            loads[part][kind].wait()
            turned = pltpu.roll(blocks[kind, part * depth:(part + 1) * depth, :],
                                lax.rem((NZ - z) * piece, width), 1).T[0:piece]

            @pl.when(home)
            def _():
                slices[0, part, kind] = turned

            @pl.when(away)
            def _():
                own[part, kind] = turned

        @pl.when(home)
        def _():
            if part == 0:
                pl.semaphore_wait(barrier, 14)
            spread(part)

        @pl.when(away)
        def _():
            if part == 0:
                pl.semaphore_wait(barrier, 18)
            cross(part).start()

    for copy in small:
        copy.wait()
    rows = lax.broadcasted_iota(jnp.int32, (16, 1), 0)
    moments = jnp.zeros((16, 1), F32)
    for row in range(16):
        moment = time_ref[pair_ref[2 * (row % 8) + row // 8]]
        moments = jnp.where(rows == row, moment, moments)
    weights[0] = jnp.exp(-energies[0] * moments)
    weights[1] = jnp.exp(energies[1] * moments)

    for part in range(PARTS):
        for kind in range(2):
            hi, lo = split(blocks[kind, part * depth:(part + 1) * depth, :])
            rhs[kind, part * depth:(part + 1) * depth, 0:width] = hi
            rhs[kind, part * depth:(part + 1) * depth, width:] = lo

        @pl.when(away)
        def _():
            cross(part).wait_recv()
            spread(part)

    def slot_of(q):
        return (block_of(q) < blk).astype(jnp.int32)

    def compute(work):
        rows = 128 * len(work)
        tiles = []
        for kind in range(2):
            for n, (q, at, u) in enumerate(work):
                for part in range(PARTS):
                    columns = slice(part * depth, (part + 1) * depth)
                    values = slices[q, part, kind]
                    factors = weights[kind, pl.ds(pl.multiple_of(u * 8, 8), 8), columns]
                    for p in range(8):
                        hi, lo = split(values * factors[p:p + 1, :])
                        lhs[kind, n * 128 + p * piece:n * 128 + (p + 1) * piece, columns] = hi
                        lhs[kind, rows + n * 128 + p * piece:rows + n * 128 + (p + 1) * piece, columns] = lo
            total = jnp.dot(lhs[kind, 0:2 * rows], rhs[kind], preferred_element_type=F32)
            tiles.append((total[0:rows, 0:width]
                          + (total[0:rows, width:] + (total[rows:, 0:width] + total[rows:, width:]))))
        product = -(tiles[0] * tiles[1])
        for n, (q, at, u) in enumerate(work):
            outgoing[at] = product[n * 128:(n + 1) * 128].reshape(NZ, piece, width)
            arrived[at, pl.ds(pl.multiple_of(z * piece, piece), piece), :] = outgoing[at, z]

    def z_copy(first, count, group, step):
        to = lax.rem(z + step, NZ)
        these = pl.ds(first, count)
        return pltpu.make_async_remote_copy(
            src_ref=outgoing.at[these, to],
            dst_ref=arrived.at[these, pl.ds(pl.multiple_of(z * piece, piece), piece)],
            send_sem=z_send.at[group], recv_sem=z_recv.at[group], device_id=z_peer(step), device_id_type=MESH)

    def share(first, count, group):
        @pl.loop(1, NZ)
        def _(step):
            z_copy(first, count, group, step).start()

    def pair(group):
        first = 2 * group
        compute([(first, first, slot_of(first)), (first + 1, first + 1, slot_of(first + 1))])
        share(first, 2, group)

    def gathered(q):
        whole = slices.at[q]
        pltpu.make_async_copy(whole, whole, ag_recv.at[q, 0]).wait()

    def relay(part):
        gather_copy(slices.at[0], 2, part, down, 2).wait_recv()
        gather_copy(slices.at[2], 3, part, sibling, 4).start()
        gather_copy(slices.at[0], 4, part, up, 1).wait_recv()
        gather_copy(slices.at[4], 5, part, sibling, 5).start()

        @pl.when(c == 1)
        def _():
            gather_copy(slices.at[2], 6, part, down, 6).start()

        @pl.when(c == 0)
        def _():
            gather_copy(slices.at[4], 6, part, up, 6).start()

    def relay_far(part):
        gather_copy(slices.at[4], 6, part, up, 6).wait_recv()
        gather_copy(slices.at[6], 7, part, sibling, 7).start()

    def receive(first, count, group):
        rest = arrived.at[pl.ds(first, count), pl.ds(0, (NZ - 1) * piece)]
        pltpu.make_async_copy(rest, rest, z_recv.at[group]).wait()

    def columns_of(k):
        return pl.ds(pl.multiple_of(k * width, width), width)

    def mirror_copy(q):
        return pltpu.make_async_remote_copy(
            src_ref=arrived.at[q], dst_ref=out_ref.at[0, slot_of(q), :, columns_of(column)],
            send_sem=mirror_send.at[q], recv_sem=mirror_recv.at[column], device_id=mirror_of(q), device_id_type=MESH)

    def place(q, at, u):
        out_ref[0, u, :, columns_of(lax.rem(block_of(q), 8))] = arrived[at].T

    def finish(group):
        first = 2 * group
        receive(first, 2, group)
        mirror_copy(first).start()
        mirror_copy(first + 1).start()
        place(first, first, slot_of(first))
        place(first + 1, first + 1, slot_of(first + 1))

    @pl.when(home)
    def _():
        compute([(0, 8, 1)])
        share(8, 1, 4)

    relay(0)
    relay(1)
    gathered(1)
    pair(0)
    relay(2)
    relay(3)
    gathered(3)
    pair(1)
    relay_far(0)
    relay_far(1)
    gathered(5)
    pair(2)
    relay_far(2)
    relay_far(3)

    @pl.when(home)
    def _():
        receive(8, 1, 4)
        place(0, 8, 1)
        receive(0, 2, 0)
        mirror_copy(1).start()
        place(0, 0, 0)
        place(1, 1, slot_of(1))

    @pl.when(away)
    def _():
        finish(0)

    gathered(7)
    pair(3)

    @pl.loop(1, 4)
    def _(group):
        finish(group)

    @pl.loop(0, 8)
    def _(k):
        @pl.when(jnp.logical_or(away, k != column))
        def _():
            into = out_ref.at[0, 0, :, columns_of(0)]
            pltpu.make_async_copy(into, into, mirror_recv.at[k]).wait()

    def sent(first, count, group):
        rest = outgoing.at[pl.ds(first, count), pl.ds(0, NZ - 1)]
        pltpu.make_async_copy(rest, rest, z_send.at[group]).wait()

    for n in range(1, 8):
        whole = slices.at[0]
        pltpu.make_async_copy(whole, whole, ag_send.at[n]).wait()

    @pl.loop(0, 4)
    def _(group):
        sent(2 * group, 2, group)

    @pl.loop(1, 8)
    def _(q):
        mirror_copy(q).wait_send()

    @pl.when(home)
    def _():
        sent(8, 1, 4)

    @pl.when(away)
    def _():
        pltpu.make_async_copy(own, own, ag_send.at[0]).wait()
        mirror_copy(0).wait_send()


def body(occupied_orbitals, empty_orbitals, occupied_energy, empty_energy, time_points, pair_table):
    states, width = occupied_orbitals.shape
    piece = width // NZ
    depth = states // PARTS
    return pl.pallas_call(
        kernel,
        out_shape=pltpu.VMEM((1, 2, width, 8 * width), F32),
        in_specs=[pl.BlockSpec(memory_space=pltpu.HBM)] * 6,
        out_specs=pl.BlockSpec(memory_space=pltpu.VMEM),
        scratch_shapes=[
            pltpu.VMEM((2, states, width), F32),
            pltpu.VMEM((2, 1, states), F32),
            pltpu.SMEM((16,), F32),
            pltpu.SMEM((16,), jnp.int32),
            pltpu.VMEM((PARTS, 2, piece, depth), F32),
            pltpu.VMEM((8, PARTS, 2, piece, depth), F32),
            pltpu.VMEM((2, states, 2 * width), BF16),
            pltpu.VMEM((2, 512, states), BF16),
            pltpu.VMEM((2, 16, states), F32),
            pltpu.VMEM((9, NZ, piece, width), F32),
            pltpu.VMEM((9, width, width), F32),
            pltpu.SemaphoreType.DMA((PARTS, 2)),
            pltpu.SemaphoreType.DMA((4,)),
            pltpu.SemaphoreType.DMA((8,)),
            pltpu.SemaphoreType.DMA((8, PARTS)),
            pltpu.SemaphoreType.DMA((5,)),
            pltpu.SemaphoreType.DMA((5,)),
            pltpu.SemaphoreType.DMA((8,)),
            pltpu.SemaphoreType.DMA((8,)),
        ],
        compiler_params=pltpu.CompilerParams(
            collective_id=0, has_side_effects=True, vmem_limit_bytes=61 * 2**20),
        cost_estimate=pl.CostEstimate(flops=2**33, bytes_accessed=2**22, transcendentals=2**16),
        name="polarizability",
    )(occupied_orbitals, empty_orbitals, occupied_energy.reshape(1, states), empty_energy.reshape(1, states),
      time_points, pair_table)


def solution(mesh):
    return jax.shard_map(
        body,
        mesh=mesh,
        in_specs=(P(None, "blk"), P(None, "blk"), P(), P(), P(), P()),
        out_specs=P("tm", None, "blk", None),
        check_vma=False,
    )
```

time: 188 us -> 42.9 us (0.23)
  the two profiles are of different devices: /device:TPU:3 before, /device:TPU:11 now
where the time goes in v2:
time: 42.9 us; the launch traced here: 42.8 us
  Pallas kernels  41.9 us (98%)
  local copies, waits for them, and re-layouts  0.97 us (2%)
    pallas_call x1, Pallas kernels, body(): pl.pallas_call(kernel, out_shape=pltpu.VMEM((1, 2, width, 8 * width), F32...  41.9 us
    unnamed x1, local copies, waits for them, and re-layouts  0.97 us

profile of v2, /device:TPU:11, one launch (start us, length us, event | category | flops | bytes accessed | tf_op | source)
XLA Modules:
  0.0 42.8 jit_solution(16880435920620217782)
XLA Ops:
  0.0 41.9 %polarizability.1 = f32[1,2,128,1024]{3,2,1,0:T(8,128)S(1)} custom-call(f32[2048,128]{1,0:T(8,128)} %occ_hbm.1, f32[2048,128]{1,0:T(8,128)} %emp_hbm.1, f32[1,2048]{1,0:T(1,128)} %bitcast.2, f32[1,2048]{1,0:T(1,128)} %bitcast.3, f32[16]{0:T(128)} %time_hbm.1, s32[16]{0:T(128)} %pair_hbm.1), custom_call_target="tpu_custom_call" | custom-call | flops 8589934592 | bytes 4194304 | tf_op jit(solution)/shard_map/polarizability/pallas_call | solution.py:309
  41.9 1.0 %copy.8 = f32[1,2,128,1024]{3,2,1,0:T(8,128)} copy(f32[1,2,128,1024]{3,2,1,0:T(8,128)S(1)} %polarizability.1) | data formatting | bytes 2097152

commit v3 on v2

--- a/solution.py
+++ b/solution.py
@@ -8,7 +8,7 @@
 MESH = pl.DeviceIdType.MESH
 NZ = 8
 NY = 4
-PARTS = 4
+PARTS = 8
 F32 = jnp.float32
 BF16 = jnp.bfloat16
 
@@ -57,7 +57,7 @@
                       for kind, ref in enumerate((emp_hbm, occ_hbm))])
     small = [pltpu.make_async_copy(source, to, small_sem.at[n]) for n, (source, to) in enumerate((
         (emp_e_hbm, energies.at[0]), (occ_e_hbm, energies.at[1]), (time_hbm, time_ref), (pair_hbm, pair_ref)))]
-    for pair in loads:
+    for pair in loads[:2]:
         for copy in pair:
             copy.start()
     for copy in small:
@@ -98,6 +98,8 @@
     for part in range(PARTS):
         for kind in range(2):
             loads[part][kind].wait()
+            if part + 2 < PARTS:
+                loads[part + 2][kind].start()
             turned = pltpu.roll(blocks[kind, part * depth:(part + 1) * depth, :],
                                 lax.rem((NZ - z) * piece, width), 1).T[0:piece]
 
@@ -166,23 +168,42 @@
             outgoing[at] = product[n * 128:(n + 1) * 128].reshape(NZ, piece, width)
             arrived[at, pl.ds(pl.multiple_of(z * piece, piece), piece), :] = outgoing[at, z]
 
+    def rows_of(plane):
+        return pl.ds(pl.multiple_of(plane * piece, piece), piece)
+
+    def far_first(n):
+        return 4 + lax.div(n + 1, 2) * (1 - 2 * lax.rem(n, 2))
+
     def z_copy(first, count, group, step):
         to = lax.rem(z + step, NZ)
         these = pl.ds(first, count)
         return pltpu.make_async_remote_copy(
-            src_ref=outgoing.at[these, to],
-            dst_ref=arrived.at[these, pl.ds(pl.multiple_of(z * piece, piece), piece)],
-            send_sem=z_send.at[group], recv_sem=z_recv.at[group], device_id=z_peer(step), device_id_type=MESH)
+            src_ref=outgoing.at[these, to], dst_ref=arrived.at[these, rows_of(z)],
+            send_sem=z_send.at[group], recv_sem=z_recv.at[group, step], device_id=z_peer(step), device_id_type=MESH)
 
     def share(first, count, group):
-        @pl.loop(1, NZ)
-        def _(step):
-            z_copy(first, count, group, step).start()
+        @pl.loop(0, NZ - 1)
+        def _(n):
+            z_copy(first, count, group, far_first(n)).start()
+
+    def columns_of(k):
+        return pl.ds(pl.multiple_of(k * width, width), width)
+
+    def mirror_copy(q, plane):
+        return pltpu.make_async_remote_copy(
+            src_ref=arrived.at[q, rows_of(plane)], dst_ref=out_ref.at[0, slot_of(q), rows_of(plane), columns_of(column)],
+            send_sem=mirror_send.at[q], recv_sem=mirror_recv.at[column], device_id=mirror_of(q), device_id_type=MESH)
 
     def pair(group):
         first = 2 * group
         compute([(first, first, slot_of(first)), (first + 1, first + 1, slot_of(first + 1))])
         share(first, 2, group)
+
+        @pl.when(jnp.logical_or(away, group > 0))
+        def _():
+            mirror_copy(first, z).start()
+
+        mirror_copy(first + 1, z).start()
 
     def gathered(q):
         whole = slices.at[q]
@@ -207,16 +228,18 @@
         gather_copy(slices.at[6], 7, part, sibling, 7).start()
 
     def receive(first, count, group):
-        rest = arrived.at[pl.ds(first, count), pl.ds(0, (NZ - 1) * piece)]
-        pltpu.make_async_copy(rest, rest, z_recv.at[group]).wait()
-
-    def columns_of(k):
-        return pl.ds(pl.multiple_of(k * width, width), width)
-
-    def mirror_copy(q):
-        return pltpu.make_async_remote_copy(
-            src_ref=arrived.at[q], dst_ref=out_ref.at[0, slot_of(q), :, columns_of(column)],
-            send_sem=mirror_send.at[q], recv_sem=mirror_recv.at[column], device_id=mirror_of(q), device_id_type=MESH)
+        @pl.loop(0, NZ - 1)
+        def _(n):
+            step = far_first(n)
+            plane = lax.rem(z + NZ - step, NZ)
+            here = arrived.at[pl.ds(first, count), rows_of(plane)]
+            pltpu.make_async_copy(here, here, z_recv.at[group, step]).wait()
+            if count == 2:
+                @pl.when(jnp.logical_or(away, group > 0))
+                def _():
+                    mirror_copy(first, plane).start()
+
+                mirror_copy(first + 1, plane).start()
 
     def place(q, at, u):
         out_ref[0, u, :, columns_of(lax.rem(block_of(q), 8))] = arrived[at].T
@@ -224,8 +247,6 @@
     def finish(group):
         first = 2 * group
         receive(first, 2, group)
-        mirror_copy(first).start()
-        mirror_copy(first + 1).start()
         place(first, first, slot_of(first))
         place(first + 1, first + 1, slot_of(first + 1))
 
@@ -234,34 +255,28 @@
         compute([(0, 8, 1)])
         share(8, 1, 4)
 
-    relay(0)
-    relay(1)
+    def each(action, parts):
+        for part in parts:
+            action(part)
+
+    early, late = range(PARTS // 2), range(PARTS // 2, PARTS)
+    each(relay, early)
     gathered(1)
     pair(0)
-    relay(2)
-    relay(3)
+    each(relay, late)
     gathered(3)
     pair(1)
-    relay_far(0)
-    relay_far(1)
+    each(relay_far, early)
     gathered(5)
     pair(2)
-    relay_far(2)
-    relay_far(3)
+    each(relay_far, late)
 
     @pl.when(home)
     def _():
         receive(8, 1, 4)
         place(0, 8, 1)
-        receive(0, 2, 0)
-        mirror_copy(1).start()
-        place(0, 0, 0)
-        place(1, 1, slot_of(1))
-
-    @pl.when(away)
-    def _():
-        finish(0)
-
+
+    finish(0)
     gathered(7)
     pair(3)
 
@@ -288,9 +303,13 @@
     def _(group):
         sent(2 * group, 2, group)
 
+    def mirrored(q):
+        whole = arrived.at[q]
+        pltpu.make_async_copy(whole, whole, mirror_send.at[q]).wait()
+
     @pl.loop(1, 8)
     def _(q):
-        mirror_copy(q).wait_send()
+        mirrored(q)
 
     @pl.when(home)
     def _():
@@ -299,7 +318,7 @@
     @pl.when(away)
     def _():
         pltpu.make_async_copy(own, own, ag_send.at[0]).wait()
-        mirror_copy(0).wait_send()
+        mirrored(0)
 
 
 def body(occupied_orbitals, empty_orbitals, occupied_energy, empty_energy, time_points, pair_table):
@@ -328,7 +347,7 @@
             pltpu.SemaphoreType.DMA((8,)),
             pltpu.SemaphoreType.DMA((8, PARTS)),
             pltpu.SemaphoreType.DMA((5,)),
-            pltpu.SemaphoreType.DMA((5,)),
+            pltpu.SemaphoreType.DMA((5, NZ)),
             pltpu.SemaphoreType.DMA((8,)),
             pltpu.SemaphoreType.DMA((8,)),
         ],

time: 42.9 us -> 40.8 us (0.951)
  the two profiles are of different devices: /device:TPU:11 before, /device:TPU:3 now
where the time goes in v3:
time: 40.8 us; the launch traced here: 40.6 us
  Pallas kernels  39.7 us (97%)
  local copies, waits for them, and re-layouts  0.97 us (2%)
    pallas_call x1, Pallas kernels, body(): pl.pallas_call(kernel, out_shape=pltpu.VMEM((1, 2, width, 8 * width), F32...  39.7 us
    unnamed x1, local copies, waits for them, and re-layouts  0.97 us

profile of v3, /device:TPU:3, one launch (start us, length us, event | category | flops | bytes accessed | tf_op | source)
XLA Modules:
  0.0 40.6 jit_solution(3209269994665012597)
XLA Ops:
  0.0 39.7 %polarizability.1 = f32[1,2,128,1024]{3,2,1,0:T(8,128)S(1)} custom-call(f32[2048,128]{1,0:T(8,128)} %occ_hbm.1, f32[2048,128]{1,0:T(8,128)} %emp_hbm.1, f32[1,2048]{1,0:T(1,128)} %bitcast.2, f32[1,2048]{1,0:T(1,128)} %bitcast.3, f32[16]{0:T(128)} %time_hbm.1, s32[16]{0:T(128)} %pair_hbm.1), custom_call_target="tpu_custom_call" | custom-call | flops 8589934592 | bytes 4194304 | tf_op jit(solution)/shard_map/polarizability/pallas_call | solution.py:328
  39.7 1.0 %copy.8 = f32[1,2,128,1024]{3,2,1,0:T(8,128)} copy(f32[1,2,128,1024]{3,2,1,0:T(8,128)S(1)} %polarizability.1) | data formatting | bytes 2097152

commit v4 on v3

v4 whole, which is shorter than its diff:
```python
import jax
import jax.numpy as jnp
from jax import lax
from jax.experimental import pallas as pl
from jax.experimental.pallas import tpu as pltpu
from jax.sharding import PartitionSpec as P

MESH = pl.DeviceIdType.MESH
NZ = 8
NY = 4
PARTS = 8
LOADS = 4
SLOTS = ((0, 0), (0, 1), (1, 0), (3, 0), (1, 1), (3, 1), (2, 0), (2, 1))
DIRECT = (0, 2, 3, 6)
DOUBLE = (7, 6)
F32 = jnp.float32
BF16 = jnp.bfloat16


def split(value):
    hi = value.astype(BF16)
    lo = (value - hi.astype(F32)).astype(BF16)
    return hi, lo


def kernel(occ_hbm, emp_hbm, occ_e_hbm, emp_e_hbm, time_hbm, pair_hbm, out_ref,
           blocks, energies, time_ref, pair_ref, slices, rhs, lhs, weights, outgoing, arrived,
           load_sem, small_sem, ag_send, ag_recv, z_send, z_recv, mirror_send, mirror_recv):
    states, width = blocks.shape[1:]
    piece = width // NZ
    depth = states // PARTS
    own = slices.at[8]
    blk, tm = lax.axis_index("blk"), lax.axis_index("tm")
    x_hi, y, c = lax.div(blk, 8), lax.rem(lax.div(blk, 2), NY), lax.rem(blk, 2)
    z, half = lax.div(tm, 2), lax.rem(tm, 2)
    home = x_hi == half
    away = jnp.logical_not(home)
    column = lax.rem(blk, 8)

    def in_column(y_to, c_to):
        return (x_hi * 8 + lax.rem(y_to, NY) * 2 + c_to, tm)

    sibling = in_column(y, 1 - c)
    up, down = in_column(y + 1, c), in_column(y + 3, c)
    across = (half * 8 + y * 2 + c, z * 2 + x_hi)

    def z_peer(step):
        return (blk, lax.rem(z + step, NZ) * 2 + half)

    def block_of(q):
        dy, flip = SLOTS[q]
        return half * 8 + lax.rem(y + dy, NY) * 2 + lax.rem(c + flip, 2)

    def mirror_of(q):
        return (block_of(q), z * 2 + x_hi)

    loads = []
    for n in range(LOADS):
        rows = pl.ds(n * (states // LOADS), states // LOADS)
        loads.append([pltpu.make_async_copy(ref.at[rows], blocks.at[kind, rows], load_sem.at[n, kind])
                      for kind, ref in enumerate((emp_hbm, occ_hbm))])
    small = [pltpu.make_async_copy(source, to, small_sem.at[n]) for n, (source, to) in enumerate((
        (emp_e_hbm, energies.at[0]), (occ_e_hbm, energies.at[1]), (time_hbm, time_ref), (pair_hbm, pair_ref)))]
    for copy in loads[0]:
        copy.start()

    barrier = pltpu.get_barrier_semaphore()

    def greet(device):
        pl.semaphore_signal(barrier, inc=1, device_id=device, device_id_type=MESH)

    @pl.loop(1, NZ)
    def _(step):
        greet(z_peer(step))

    for q in range(1, 8):
        if q not in DOUBLE:
            greet(mirror_of(q))

    @pl.when(away)
    def _():
        greet(across)
        greet(sibling)
        greet(up)
        greet(down)

    for pair in loads[1:]:
        for copy in pair:
            copy.start()
    for copy in small:
        copy.start()

    def gather_copy(source, at, part, device, n):
        return pltpu.make_async_remote_copy(
            src_ref=source.at[part], dst_ref=slices.at[at, part], send_sem=ag_send.at[n],
            recv_sem=ag_recv.at[at, part if at in DIRECT else 0], device_id=device, device_id_type=MESH)

    def cross(part):
        return gather_copy(own, 0, part, across, 0)

    def spread(part):
        for at, device, n in ((3, up, 1), (2, down, 2), (1, sibling, 3)):
            gather_copy(slices.at[0], at, part, device, n).start()

    mine = jnp.where(home, 0, 8)
    run = PARTS // LOADS
    for n in range(LOADS):
        for kind in range(2):
            loads[n][kind].wait()
        for kind in range(2):
            for part in range(n * run, (n + 1) * run):
                rows = slice(part * depth, (part + 1) * depth)
                turned = pltpu.roll(blocks[kind, rows, :], lax.rem((NZ - z) * piece, width), 1).T
                slices[mine, part, kind] = turned[0:piece]
        if n == 0:
            pl.semaphore_wait(barrier, jnp.where(home, 14, 18) - len(DOUBLE))

        @pl.when(home)
        def _():
            for part in range(n * run, (n + 1) * run):
                spread(part)

        @pl.when(away)
        def _():
            for part in range(n * run, (n + 1) * run):
                cross(part).start()

        for kind in range(2):
            rows = slice(n * run * depth, (n + 1) * run * depth)
            hi, lo = split(blocks[kind, rows, :])
            rhs[kind, rows, 0:width] = hi
            rhs[kind, rows, width:] = lo

    for copy in small:
        copy.wait()
    rows = lax.broadcasted_iota(jnp.int32, (16, 1), 0)
    moments = jnp.zeros((16, 1), F32)
    for row in range(16):
        moment = time_ref[pair_ref[2 * (row % 8) + row // 8]]
        moments = jnp.where(rows == row, moment, moments)
    weights[0] = jnp.exp(-energies[0] * moments)
    weights[1] = jnp.exp(energies[1] * moments)

    @pl.when(away)
    def _():
        for part in range(PARTS):
            cross(part).wait_recv()
            spread(part)

    def slot_of(q):
        return (block_of(q) < blk).astype(jnp.int32)

    def compute(work):
        rows = 128 * len(work)
        tiles = []
        for kind in range(2):
            for n, (q, at, u) in enumerate(work):
                for part in range(PARTS):
                    columns = slice(part * depth, (part + 1) * depth)
                    values = slices[q, part, kind]
                    factors = weights[kind, pl.ds(pl.multiple_of(u * 8, 8), 8), columns]
                    for p in range(8):
                        hi, lo = split(values * factors[p:p + 1, :])
                        lhs[kind, n * 128 + p * piece:n * 128 + (p + 1) * piece, columns] = hi
                        lhs[kind, rows + n * 128 + p * piece:rows + n * 128 + (p + 1) * piece, columns] = lo
            total = jnp.dot(lhs[kind, 0:2 * rows], rhs[kind], preferred_element_type=F32)
            tiles.append((total[0:rows, 0:width]
                          + (total[0:rows, width:] + (total[rows:, 0:width] + total[rows:, width:]))))
        product = -(tiles[0] * tiles[1])
        for n, (q, at, u) in enumerate(work):
            outgoing[at] = product[n * 128:(n + 1) * 128].reshape(NZ, piece, width)
            arrived[at, pl.ds(pl.multiple_of(z * piece, piece), piece), :] = outgoing[at, z]

    def rows_of(plane):
        return pl.ds(pl.multiple_of(plane * piece, piece), piece)

    def far_first(n):
        return 4 + lax.div(n + 1, 2) * (1 - 2 * lax.rem(n, 2))

    def z_copy(first, count, step):
        to = lax.rem(z + step, NZ)
        these = pl.ds(first, count)
        return pltpu.make_async_remote_copy(
            src_ref=outgoing.at[these, to], dst_ref=arrived.at[these, rows_of(z)],
            send_sem=z_send.at[first], recv_sem=z_recv.at[first, step], device_id=z_peer(step), device_id_type=MESH)

    def share(first, count):
        @pl.loop(0, NZ - 1)
        def _(n):
            z_copy(first, count, far_first(n)).start()

    def columns_of(k):
        return pl.ds(pl.multiple_of(k * width, width), width)

    def mirror_copy(q, plane):
        return pltpu.make_async_remote_copy(
            src_ref=arrived.at[q, rows_of(plane)], dst_ref=out_ref.at[0, slot_of(q), rows_of(plane), columns_of(column)],
            send_sem=mirror_send.at[q], recv_sem=mirror_recv.at[column], device_id=mirror_of(q), device_id_type=MESH)

    def mirror(q, plane):
        if q in DOUBLE:
            return
        if q == 0:
            pl.when(away)(mirror_copy(q, plane).start)
        else:
            mirror_copy(q, plane).start()

    def gathered(q):
        whole = slices.at[q]
        pltpu.make_async_copy(whole, whole, ag_recv.at[q, 0]).wait()

    def relay(part):
        gather_copy(slices.at[0], 2, part, down, 2).wait_recv()
        gather_copy(slices.at[2], 4, part, sibling, 4).start()
        gather_copy(slices.at[0], 3, part, up, 1).wait_recv()
        gather_copy(slices.at[3], 5, part, sibling, 5).start()

        @pl.when(c == 1)
        def _():
            gather_copy(slices.at[2], 6, part, down, 6).start()

        @pl.when(c == 0)
        def _():
            gather_copy(slices.at[3], 6, part, up, 6).start()

    def relay_far(part):
        gather_copy(slices.at[3], 6, part, up, 6).wait_recv()
        gather_copy(slices.at[6], 7, part, sibling, 7).start()

    def receive(first, count):
        @pl.loop(0, NZ - 1)
        def _(n):
            step = far_first(n)
            plane = lax.rem(z + NZ - step, NZ)
            here = arrived.at[pl.ds(first, count), rows_of(plane)]
            pltpu.make_async_copy(here, here, z_recv.at[first, step]).wait()
            for q in range(first, first + count):
                if q < 8:
                    mirror(q, plane)

    def place(q, at, u):
        out_ref[0, u, :, columns_of(lax.rem(block_of(q), 8))] = arrived[at].T

    def work(at):
        q = at if at < 8 else (0, 7, 6)[at - 8]
        u = slot_of(q)
        return (q, at, u if at < 8 else 1 - u)

    def make(first, count):
        compute([work(at) for at in range(first, first + count)])
        share(first, count)
        for q in range(first, first + count):
            if q < 8:
                mirror(q, z)

    def finish(first, count):
        receive(first, count)
        for at in range(first, first + count):
            place(*work(at))

    def each(action, parts):
        for part in parts:
            action(part)

    early, late = range(PARTS // 2), range(PARTS // 2, PARTS)

    @pl.when(home)
    def _():
        compute([work(0), work(8)])
        share(0, 1)
        share(8, 1)

    each(relay, early)

    @pl.when(away)
    def _():
        make(0, 1)

    gathered(1)
    make(1, 1)
    each(relay, late)
    make(2, 2)
    each(relay_far, early)
    gathered(4)
    gathered(5)
    make(4, 2)
    finish(0, 1)
    finish(1, 1)

    @pl.when(home)
    def _():
        finish(8, 1)

    each(relay_far, late)
    make(6, 1)
    if 6 in DOUBLE:
        make(10, 1)
    gathered(7)
    make(7, 1)
    if 7 in DOUBLE:
        make(9, 1)
    finish(2, 2)
    finish(4, 2)
    finish(6, 1)
    if 6 in DOUBLE:
        finish(10, 1)
    finish(7, 1)
    if 7 in DOUBLE:
        finish(9, 1)

    for q in range(8):
        if q in DOUBLE:
            continue

        def mirror_arrival(q=q):
            into = out_ref.at[0, 0, :, columns_of(0)]
            pltpu.make_async_copy(into, into, mirror_recv.at[lax.rem(block_of(q), 8)]).wait()
            whole = arrived.at[q]
            pltpu.make_async_copy(whole, whole, mirror_send.at[q]).wait()

        if q == 0:
            pl.when(away)(mirror_arrival)
        else:
            mirror_arrival()

    def sent(first, count):
        rest = outgoing.at[pl.ds(first, count), pl.ds(0, NZ - 1)]
        pltpu.make_async_copy(rest, rest, z_send.at[first]).wait()

    for n in range(1, 8):
        whole = slices.at[0]
        pltpu.make_async_copy(whole, whole, ag_send.at[n]).wait()

    for first, count in ((0, 1), (1, 1), (2, 2), (4, 2), (6, 1), (7, 1)):
        sent(first, count)
    for q in DOUBLE:
        sent({7: 9, 6: 10}[q], 1)

    @pl.when(home)
    def _():
        sent(8, 1)

    @pl.when(away)
    def _():
        pltpu.make_async_copy(own, own, ag_send.at[0]).wait()


def body(occupied_orbitals, empty_orbitals, occupied_energy, empty_energy, time_points, pair_table):
    states, width = occupied_orbitals.shape
    piece = width // NZ
    depth = states // PARTS
    return pl.pallas_call(
        kernel,
        out_shape=pltpu.VMEM((1, 2, width, 8 * width), F32),
        in_specs=[pl.BlockSpec(memory_space=pltpu.HBM)] * 6,
        out_specs=pl.BlockSpec(memory_space=pltpu.VMEM),
        scratch_shapes=[
            pltpu.VMEM((2, states, width), F32),
            pltpu.VMEM((2, 1, states), F32),
            pltpu.SMEM((16,), F32),
            pltpu.SMEM((16,), jnp.int32),
            pltpu.VMEM((9, PARTS, 2, piece, depth), F32),
            pltpu.VMEM((2, states, 2 * width), BF16),
            pltpu.VMEM((2, 512, states), BF16),
            pltpu.VMEM((2, 16, states), F32),
            pltpu.VMEM((11, NZ, piece, width), F32),
            pltpu.VMEM((11, width, width), F32),
            pltpu.SemaphoreType.DMA((LOADS, 2)),
            pltpu.SemaphoreType.DMA((4,)),
            pltpu.SemaphoreType.DMA((8,)),
            pltpu.SemaphoreType.DMA((8, PARTS)),
            pltpu.SemaphoreType.DMA((11,)),
            pltpu.SemaphoreType.DMA((11, NZ)),
            pltpu.SemaphoreType.DMA((8,)),
            pltpu.SemaphoreType.DMA((8,)),
        ],
        compiler_params=pltpu.CompilerParams(
            collective_id=0, has_side_effects=True, vmem_limit_bytes=61 * 2**20),
        cost_estimate=pl.CostEstimate(flops=2**33, bytes_accessed=2**22, transcendentals=2**16),
        name="polarizability",
    )(occupied_orbitals, empty_orbitals, occupied_energy.reshape(1, states), empty_energy.reshape(1, states),
      time_points, pair_table)


def solution(mesh):
    return jax.shard_map(
        body,
        mesh=mesh,
        in_specs=(P(None, "blk"), P(None, "blk"), P(), P(), P(), P()),
        out_specs=P("tm", None, "blk", None),
        check_vma=False,
    )
```

time: 40.8 us -> 37.6 us (0.922)
  Pallas kernels: 39.7 us -> 36.5 us
    pallas_call x1, Pallas kernels: 39.7 us -> 36.5 us  [body(): pl.pallas_call(kernel, out_shape=pltpu.VMEM((1, 2, width, 8 * width), F32...]
where the time goes in v4:
time: 37.6 us; the launch traced here: 37.5 us
  Pallas kernels  36.5 us (97%)
  local copies, waits for them, and re-layouts  0.97 us (3%)
    pallas_call x1, Pallas kernels, body(): pl.pallas_call(kernel, out_shape=pltpu.VMEM((1, 2, width, 8 * width), F32...  36.5 us
    unnamed x1, local copies, waits for them, and re-layouts  0.97 us

profile of v4, /device:TPU:3, one launch (start us, length us, event | category | flops | bytes accessed | tf_op | source)
XLA Modules:
  0.0 37.5 jit_solution(12196588776920550328)
XLA Ops:
  0.0 36.5 %polarizability.1 = f32[1,2,128,1024]{3,2,1,0:T(8,128)S(1)} custom-call(f32[2048,128]{1,0:T(8,128)} %occ_hbm.1, f32[2048,128]{1,0:T(8,128)} %emp_hbm.1, f32[1,2048]{1,0:T(1,128)} %bitcast.2, f32[1,2048]{1,0:T(1,128)} %bitcast.3, f32[16]{0:T(128)} %time_hbm.1, s32[16]{0:T(128)} %pair_hbm.1), custom_call_target="tpu_custom_call" | custom-call | flops 8589934592 | bytes 4194304 | tf_op jit(solution)/shard_map/polarizability/pallas_call | solution.py:352
  36.5 1.0 %copy.8 = f32[1,2,128,1024]{3,2,1,0:T(8,128)} copy(f32[1,2,128,1024]{3,2,1,0:T(8,128)S(1)} %polarizability.1) | data formatting | bytes 2097152

commit v5 on v4

--- a/solution.py
+++ b/solution.py
@@ -13,6 +13,7 @@
 SLOTS = ((0, 0), (0, 1), (1, 0), (3, 0), (1, 1), (3, 1), (2, 0), (2, 1))
 DIRECT = (0, 2, 3, 6)
 DOUBLE = (7, 6)
+PLACES = (0, 1, 2, 3, 4, 5, 6, 6, 7, 7, 0)
 F32 = jnp.float32
 BF16 = jnp.bfloat16
 
@@ -235,22 +236,22 @@
             here = arrived.at[pl.ds(first, count), rows_of(plane)]
             pltpu.make_async_copy(here, here, z_recv.at[first, step]).wait()
             for q in range(first, first + count):
-                if q < 8:
+                if q < 6:
                     mirror(q, plane)
 
     def place(q, at, u):
         out_ref[0, u, :, columns_of(lax.rem(block_of(q), 8))] = arrived[at].T
 
     def work(at):
-        q = at if at < 8 else (0, 7, 6)[at - 8]
+        q = PLACES[at]
         u = slot_of(q)
-        return (q, at, u if at < 8 else 1 - u)
+        return (q, at, 1 - u if at in (7, 9, 10) else u)
 
     def make(first, count):
         compute([work(at) for at in range(first, first + count)])
         share(first, count)
         for q in range(first, first + count):
-            if q < 8:
+            if q < 6:
                 mirror(q, z)
 
     def finish(first, count):
@@ -266,47 +267,47 @@
 
     @pl.when(home)
     def _():
-        compute([work(0), work(8)])
+        compute([work(0), work(10)])
         share(0, 1)
-        share(8, 1)
+        share(10, 1)
+
+    @pl.when(away)
+    def _():
+        make(0, 1)
+
+    @pl.when(home)
+    def _():
+        gathered(1)
+        make(1, 1)
 
     each(relay, early)
 
     @pl.when(away)
     def _():
-        make(0, 1)
-
-    gathered(1)
-    make(1, 1)
+        gathered(1)
+        make(1, 1)
+
     each(relay, late)
     make(2, 2)
     each(relay_far, early)
     gathered(4)
     gathered(5)
     make(4, 2)
+    each(relay_far, late)
+    make(6, 2)
     finish(0, 1)
     finish(1, 1)
 
     @pl.when(home)
     def _():
-        finish(8, 1)
-
-    each(relay_far, late)
-    make(6, 1)
-    if 6 in DOUBLE:
-        make(10, 1)
+        finish(10, 1)
+
     gathered(7)
-    make(7, 1)
-    if 7 in DOUBLE:
-        make(9, 1)
+    make(8, 2)
     finish(2, 2)
     finish(4, 2)
-    finish(6, 1)
-    if 6 in DOUBLE:
-        finish(10, 1)
-    finish(7, 1)
-    if 7 in DOUBLE:
-        finish(9, 1)
+    finish(6, 2)
+    finish(8, 2)
 
     for q in range(8):
         if q in DOUBLE:
@@ -331,14 +332,12 @@
         whole = slices.at[0]
         pltpu.make_async_copy(whole, whole, ag_send.at[n]).wait()
 
-    for first, count in ((0, 1), (1, 1), (2, 2), (4, 2), (6, 1), (7, 1)):
+    for first, count in ((0, 1), (1, 1), (2, 2), (4, 2), (6, 2), (8, 2)):
         sent(first, count)
-    for q in DOUBLE:
-        sent({7: 9, 6: 10}[q], 1)
 
     @pl.when(home)
     def _():
-        sent(8, 1)
+        sent(10, 1)
 
     @pl.when(away)
     def _():

time: 37.6 us -> 36.8 us (0.979)
  Pallas kernels: 36.5 us -> 35.7 us
    pallas_call x1, Pallas kernels: 36.5 us -> 35.7 us  [body(): pl.pallas_call(kernel, out_shape=pltpu.VMEM((1, 2, width, 8 * width), F32...]
where the time goes in v5:
time: 36.8 us; the launch traced here: 36.7 us
  Pallas kernels  35.7 us (97%)
  local copies, waits for them, and re-layouts  0.97 us (3%)
    pallas_call x1, Pallas kernels, body(): pl.pallas_call(kernel, out_shape=pltpu.VMEM((1, 2, width, 8 * width), F32...  35.7 us
    unnamed x1, local copies, waits for them, and re-layouts  0.97 us

profile of v5, /device:TPU:3, one launch (start us, length us, event | category | flops | bytes accessed | tf_op | source)
XLA Modules:
  0.0 36.7 jit_solution(6458501555967817338)
XLA Ops:
  0.0 35.7 %polarizability.1 = f32[1,2,128,1024]{3,2,1,0:T(8,128)S(1)} custom-call(f32[2048,128]{1,0:T(8,128)} %occ_hbm.1, f32[2048,128]{1,0:T(8,128)} %emp_hbm.1, f32[1,2048]{1,0:T(1,128)} %bitcast.2, f32[1,2048]{1,0:T(1,128)} %bitcast.3, f32[16]{0:T(128)} %time_hbm.1, s32[16]{0:T(128)} %pair_hbm.1), custom_call_target="tpu_custom_call" | custom-call | flops 8589934592 | bytes 4194304 | tf_op jit(solution)/shard_map/polarizability/pallas_call | solution.py:351
  35.7 1.0 %copy.8 = f32[1,2,128,1024]{3,2,1,0:T(8,128)} copy(f32[1,2,128,1024]{3,2,1,0:T(8,128)S(1)} %polarizability.1) | data formatting | bytes 2097152

commit v6 on v5

--- a/solution.py
+++ b/solution.py
@@ -186,9 +186,8 @@
             send_sem=z_send.at[first], recv_sem=z_recv.at[first, step], device_id=z_peer(step), device_id_type=MESH)
 
     def share(first, count):
-        @pl.loop(0, NZ - 1)
-        def _(n):
-            z_copy(first, count, far_first(n)).start()
+        for step in (4, 3, 5, 2, 6, 1, 7):
+            z_copy(first, count, step).start()
 
     def columns_of(k):
         return pl.ds(pl.multiple_of(k * width, width), width)
@@ -303,8 +302,8 @@
         finish(10, 1)
 
     gathered(7)
+    finish(2, 2)
     make(8, 2)
-    finish(2, 2)
     finish(4, 2)
     finish(6, 2)
     finish(8, 2)

time: 36.8 us -> 36.8 us (level)
  no operation moved by 1% of the time
where the time goes in v6:
time: 36.8 us; the launch traced here: 36.7 us
  Pallas kernels  35.8 us (97%)
  local copies, waits for them, and re-layouts  0.97 us (3%)
    pallas_call x1, Pallas kernels, body(): pl.pallas_call(kernel, out_shape=pltpu.VMEM((1, 2, width, 8 * width), F32...  35.8 us
    unnamed x1, local copies, waits for them, and re-layouts  0.97 us

profile of v6, /device:TPU:3, one launch (start us, length us, event | category | flops | bytes accessed | tf_op | source)
XLA Modules:
  0.0 36.7 jit_solution(17544158350398350013)
XLA Ops:
  0.0 35.8 %polarizability.1 = f32[1,2,128,1024]{3,2,1,0:T(8,128)S(1)} custom-call(f32[2048,128]{1,0:T(8,128)} %occ_hbm.1, f32[2048,128]{1,0:T(8,128)} %emp_hbm.1, f32[1,2048]{1,0:T(1,128)} %bitcast.2, f32[1,2048]{1,0:T(1,128)} %bitcast.3, f32[16]{0:T(128)} %time_hbm.1, s32[16]{0:T(128)} %pair_hbm.1), custom_call_target="tpu_custom_call" | custom-call | flops 8589934592 | bytes 4194304 | tf_op jit(solution)/shard_map/polarizability/pallas_call | solution.py:350
  35.8 1.0 %copy.8 = f32[1,2,128,1024]{3,2,1,0:T(8,128)} copy(f32[1,2,128,1024]{3,2,1,0:T(8,128)S(1)} %polarizability.1) | data formatting | bytes 2097152
